TPU v7x, 768 devices: a whole 4x8x12 slice. The times are simulated.
768 devices in a mesh: batch: 128 (over y, x, z_hi, core), tower: 6 (over z_lo).
Axes of the slice: x: 4, y: 8, z: 12 (z_hi: 2, z_lo: 6; z = z_hi * 6 + z_lo), core: 2. Of those that a mesh axis runs over, the one named last changes fastest.
Arguments:
- image_features: bfloat16 [18432, 1152], P('batch', 'tower'), may hold values from -6 to 6
- text_features: bfloat16 [18432, 1152], P('batch', 'tower'), may hold values from -6 to 6
- image_head: bfloat16 [1152, 1152], P('tower'), may hold values from -0.1875 to 0.1875
- text_head: bfloat16 [1152, 1152], P('tower'), may hold values from -0.1875 to 0.1875
- caption_ids: int32 [18432], replicated, may hold values from 0 to 9215
- logit_scale: float32 [1], replicated, may hold values from 5 to 20
- logit_bias: float32 [1], replicated, may hold values from -4 to -1
Outputs:
- loss: float32 [1], replicated
- image_head_grad: float32 [1152, 1152], P('tower')
- text_head_grad: float32 [1152, 1152], P('tower')
Inputs may be any that keep to these rules, and one draw needn't show every extreme that they name: `caption_ids`: image and caption of slots with equal ids count as matching pairs.
All inputs are finite; a program needn't handle non-finite values.
Results may differ from a plain program's by a relative error of at most 0.0033.
Values may be sent and summed in bfloat16 or wider, within the bound.
A program may use at most 64 MiB of HBM per device.

v0:
```python
import jax
import jax.numpy as jnp
from jax import lax
from jax.sharding import PartitionSpec as P

norm_eps = 1e-06


def normalize(unscaled):
    inverse = lax.rsqrt(jnp.sum(unscaled * unscaled, axis=-1, keepdims=True) + norm_eps)
    return (unscaled * inverse, inverse)


def backward_norm(grad, unit, inverse):
    return (inverse * (grad - unit * jnp.sum(unit * grad, axis=-1, keepdims=True))).astype(
        jnp.bfloat16
    )


def signed_logits(image_rows, image_ids, text_rows, text_ids, logit_mult, logit_shift):
    inner = lax.dot_general(
        image_rows, text_rows, (((1,), (1,)), ((), ())), preferred_element_type=jnp.float32
    )
    logits = logit_mult * inner + logit_shift
    sign_table = jnp.where(image_ids[:, None] == text_ids[None, :], 1.0, -1.0).astype(jnp.float32)
    return (logits, sign_table)


def coefficients(logits, sign_table, logit_mult, pair_total):
    return (-(sign_table * logit_mult / pair_total) * jax.nn.sigmoid(-sign_table * logits)).astype(
        jnp.bfloat16
    )


def transpose_product(left, right):
    return lax.dot_general(
        left, right, (((0,), (0,)), ((), ())), preferred_element_type=jnp.float32
    )


def on_device(
    image_features, text_features, image_head, text_head, caption_ids, logit_scale, logit_bias
):
    row_count = image_features.shape[0]
    tower_count = lax.axis_size("tower")
    batch_count = lax.axis_size("batch")
    block_rows = row_count // tower_count
    my_tower = lax.axis_index("tower")
    my_batch = lax.axis_index("batch")
    pair_total = caption_ids.shape[0]
    logit_mult = logit_scale[0]
    logit_shift = logit_bias[0]
    image_partial = jnp.dot(image_features, image_head, preferred_element_type=jnp.float32)
    text_partial = jnp.dot(text_features, text_head, preferred_element_type=jnp.float32)
    image_raw, text_raw = lax.psum((image_partial, text_partial), "tower")
    image_unit, image_inverse = normalize(image_raw)
    text_unit, text_inverse = normalize(text_raw)
    image_embed = image_unit.astype(jnp.bfloat16)
    text_embed = text_unit.astype(jnp.bfloat16)
    text_share = lax.dynamic_slice_in_dim(text_embed, my_tower * block_rows, block_rows, 0)
    image_share = lax.dynamic_slice_in_dim(image_embed, my_tower * block_rows, block_rows, 0)
    group_ids = lax.dynamic_slice_in_dim(caption_ids, my_batch * row_count, row_count, 0)
    id_table = caption_ids.reshape(batch_count, row_count)
    share_ids = lax.dynamic_slice_in_dim(id_table, my_tower * block_rows, block_rows, 1).reshape(-1)
    all_text, all_image = (
        lax.all_gather(text_share, "batch", axis=0, tiled=True),
        lax.all_gather(image_share, "batch", axis=0, tiled=True),
    )
    loss_acc = jnp.zeros((), jnp.float32)
    logits, sign_table = signed_logits(
        image_embed, group_ids, all_text, share_ids, logit_mult, logit_shift
    )
    loss_acc = loss_acc - jnp.sum(jax.nn.log_sigmoid(sign_table * logits)) / pair_total
    pair_coef = coefficients(logits, sign_table, logit_mult, pair_total)
    image_acc = jnp.dot(pair_coef, all_text, preferred_element_type=jnp.float32)
    back_logits, back_sign = signed_logits(
        all_image, share_ids, text_embed, group_ids, logit_mult, logit_shift
    )
    back_coef = coefficients(back_logits, back_sign, logit_mult, pair_total)
    text_acc = transpose_product(back_coef, all_image)
    image_grad, text_grad, group_loss = lax.psum((image_acc, text_acc, loss_acc), "tower")
    image_delta = backward_norm(image_grad, image_unit, image_inverse)
    text_delta = backward_norm(text_grad, text_unit, text_inverse)
    image_head_part = transpose_product(image_features, image_delta)
    text_head_part = transpose_product(text_features, text_delta)
    image_head_grad, text_head_grad, loss_value = lax.psum(
        (image_head_part, text_head_part, group_loss), "batch"
    )
    return (loss_value.reshape(1), image_head_grad, text_head_grad)


def solution(mesh):
    placed = (
        P("batch", "tower"),
        P("batch", "tower"),
        P("tower", None),
        P("tower", None),
        P(),
        P(),
        P(),
    )
    return jax.shard_map(
        on_device,
        mesh=mesh,
        in_specs=placed,
        out_specs=(P(), P("tower", None), P("tower", None)),
        check_vma=False,
    )
```

profile of v0, /device:TPU:1, one launch (start us, length us, event | category | flops | bytes accessed | tf_op | source)
XLA Modules:
  0.0 2427.1 jit_solution(559130744360710312)
XLA Ops:
  7.2 1.0 copy-done
  8.2 2.0 fusion.48
  10.2 2.1 fusion.49
  12.3 0.0 all-gather.3.cloned.1.call-start
  12.4 106.5 %all-reduce.11.cloned.1.call-done = (f32[144,1152]{1,0:T(8,128)}, f32[144,1152]{1,0:T(8,128)}) async-done(((f32[144,1152]{1,0:T(8,128)}, f32[144,1152]{1,0:T(8,128)}), (f32[144,1152]{1,0:T(8,128)}, f32[144,1152]{1,0:T(8,128)})) %all-reduce.11.cloned.1.call-update) | async-done | bytes 1327120 | tf_op jit(solution)/shard_map/psum | solution.py:55
  118.9 1.3 multiply_reduce_fusion.2
  120.2 1.2 multiply_convert_fusion.2
  121.4 0.6 constant_dynamic-slice_fusion.1
  122.0 0.0 all-gather.5.cloned.1.call-start
  122.1 0.1 multiply_reduce_fusion.3
  122.2 0.1 multiply_convert_fusion.3
  122.3 0.6 constant_dynamic-slice_fusion
  123.0 0.0 all-reduce.9.cloned.1.call-start
  123.1 0.1 reshape.30
  123.2 0.1 constant_dynamic-slice_fusion.2
  123.3 0.1 eq.29
  123.4 0.1 dynamic_slice.12
  124.8 179.7 %all-gather.3.cloned.1.call-done = bf16[3072,1152]{1,0:T(8,128)(2,1)} async-done(((bf16[24,1152]{1,0:T(8,128)(2,1)}), bf16[3072,1152]{1,0:T(8,128)(2,1)}) %all-gather.3.cloned.1.call-update) | async-done | bytes 7077904 | tf_op jit(solution)/shard_map/all_gather | solution.py:66
  304.5 7.0 fusion.21
  311.5 2.5 fusion.23
  313.9 166.7 %all-gather.5.cloned.1.call-done = bf16[3072,1152]{1,0:T(8,128)(2,1)} async-done(((bf16[24,1152]{1,0:T(8,128)(2,1)}), bf16[3072,1152]{1,0:T(8,128)(2,1)}) %all-gather.5.cloned.1.call-update) | async-done | bytes 7077904 | tf_op jit(solution)/shard_map/all_gather | solution.py:67
  480.6 9.6 fusion.22
  490.2 0.0 all-reduce.7.cloned.1.call-start
  490.2 89.6 %all-reduce.9.cloned.1.call-done = (f32[144,1152]{1,0:T(8,128)}, f32[144,1152]{1,0:T(8,128)}) async-done(((f32[144,1152]{1,0:T(8,128)}, f32[144,1152]{1,0:T(8,128)}), (f32[144,1152]{1,0:T(8,128)}, f32[144,1152]{1,0:T(8,128)})) %all-reduce.9.cloned.1.call-update) | async-done | bytes 1327120 | tf_op jit(solution)/shard_map/psum | solution.py:81
  579.9 1.6 multiply_reduce_fusion
  581.5 1.3 convolution_bitcast_fusion.1
  582.9 1.3 convolution_bitcast_fusion
  584.9 17.4 psum.58
  602.4 484.8 %psum.59 = f32[1]{0:T(128)} all-reduce(f32[1]{0:T(128)} %bitcast.2), channel_id=1, replica_groups=mesh['batch'=128,'tower'=6] {'batch'}, use_global_device_ids=true, to_apply=%region_6.7 | all-reduce | flops 1 | bytes 8 | tf_op jit(solution)/shard_map/psum | solution.py:86
  1087.1 1330.3 %all-reduce.7.cloned.1.call-done = (f32[192,1152]{1,0:T(8,128)}, f32[192,1152]{1,0:T(8,128)}) async-done(((f32[192,1152]{1,0:T(8,128)}, f32[192,1152]{1,0:T(8,128)}), (f32[192,1152]{1,0:T(8,128)}, f32[192,1152]{1,0:T(8,128)})) %all-reduce.7.cloned.1.call-update) | async-done | bytes 1769488 | tf_op jit(solution)/shard_map/psum | solution.py:86
  2417.5 2.2 copy.18
  2419.7 0.9 copy.19
  (27 shorter events, 0.2 us)
Async XLA Ops:
  7.2 1.0 copy-start
  7.2 111.7 %all-reduce.11.cloned.1.call-start = ((), (), s32[]{:S(2)}) async-start(), calls=%async_computation.4 | async-start | bytes 2654208 | tf_op jit(solution)/shard_map/psum | solution.py:55
  12.3 292.1 %all-gather.3.cloned.1.call-start = ((), (), s32[]{:S(2)}) async-start(), calls=%async_computation | async-start | bytes 7133184 | tf_op jit(solution)/shard_map/all_gather | solution.py:66
  118.9 3.2 copy-start.2
  118.9 4.2 copy-start.8
  122.0 358.6 %all-gather.5.cloned.1.call-start = ((), (), s32[]{:S(2)}) async-start(), calls=%async_computation.1 | async-start | bytes 7133184 | tf_op jit(solution)/shard_map/all_gather | solution.py:67
  123.0 456.9 %all-reduce.9.cloned.1.call-start = ((), (), s32[]{:S(2)}) async-start(), calls=%async_computation.3 | async-start | bytes 2654208 | tf_op jit(solution)/shard_map/psum | solution.py:81
  304.5 7.0 copy-start.9
  490.2 89.7 %copy-start.1 = (f32[144,1152]{1,0:T(8,128)S(1)}, f32[144,1152]{1,0:T(8,128)}, u32[]{:S(2)}) copy-start(f32[144,1152]{1,0:T(8,128)} %get-tuple-element.8) | copy-start | bytes 1990660
  490.2 91.4 %copy-start.6 = (bf16[144,192]{1,0:T(8,128)(2,1)S(1)}, bf16[144,192]{1,0:T(8,128)(2,1)}, u32[]{:S(2)}) copy-start(bf16[144,192]{1,0:T(8,128)(2,1)} %param.7) | copy-start | bytes 165892
  490.2 1927.3 %all-reduce.7.cloned.1.call-start = ((), (), s32[]{:S(2)}) async-start(), calls=%async_computation.2 | async-start | bytes 3538944 | tf_op jit(solution)/shard_map/psum | solution.py:86
  579.9 1.7 copy-start.4
  581.5 1.4 copy-start.3
  581.5 1.4 copy-start.7
  2417.5 2.2 copy-start.5
Sparse Core Ops, SparseCore 0:
  12.5 106.3 all-reduce.10
  124.9 179.5 all-gather.2
  310.5 170.0 all-gather.4
  490.3 89.4 all-reduce.8
  584.4 1833.0 all-reduce.6
where the time goes:
time: 2430 us
  waiting for transfers between devices  1870 us (77%)
  blocking collectives  502 us (21%)
  matrix products  25.8 us (1%)
    psum x1, waiting for transfers between devices, on_device(): lax.psum((image_head_part, text_head_part, group_loss), 'batch')  1330 us
    psum x1, blocking collectives, on_device(): lax.psum((image_head_part, text_head_part, group_loss), 'batch')  485 us
    all_gather x1, waiting for transfers between devices, on_device(): lax.all_gather(text_share, 'batch', axis=0, tiled=True)  180 us
    all_gather x1, waiting for transfers between devices, on_device(): lax.all_gather(image_share, 'batch', axis=0, tiled=True)  167 us
    psum x1, waiting for transfers between devices, on_device(): image_raw, text_raw = lax.psum((image_partial, text_partial), 'tower')  106 us
    psum x1, waiting for transfers between devices, on_device(): lax.psum((image_acc, text_acc, loss_acc), 'tower')  89.6 us
  transfers between devices with their start and end apart: 5, of which 5 were waited for; matrix products, arithmetic and copies ran while one was open for 0% of the time, Pallas kernels for 0%

commit v1 on v0

v1 whole, which is shorter than its diff:
```python
import functools

import jax
import jax.numpy as jnp
from jax import lax
from jax.experimental import pallas as pl
from jax.experimental.pallas import tpu as pltpu
from jax.sharding import PartitionSpec as P

MESH = pl.DeviceIdType.MESH
F32, BF16 = jnp.float32, jnp.bfloat16
NX, NY, NZ, NT = 4, 8, 12, 6
E = 1152
U = 48
NI, NJ = NZ * U, 4 * NX * U
norm_eps = 1e-06


def place():
    b = lax.axis_index("batch")
    zl = lax.axis_index("tower")
    c = lax.rem(b, 2)
    zh = lax.rem(b // 2, 2)
    x = lax.rem(b // 4, NX)
    y = b // 16
    return x, y, zh, zl, c


def device(x, y, z, c):
    return (((y * NX + x) * 2 + z // NT) * 2 + c, lax.rem(z, NT))


def rows(i, n=U):
    return pl.ds(pl.multiple_of(i * n, 8 if n % 16 else 16), n)


def copy(src, dst, ss, rs, dev):
    return pltpu.make_async_remote_copy(
        src_ref=src, dst_ref=dst, send_sem=ss, recv_sem=rs, device_id=dev, device_id_type=MESH
    )


def kernel(
    fi, ft, hi, ht, ids_i, ids_t, scale, bias,
    out, loss_out,
    h, fx, fa, part, spart, rpart, unit, inv,
    img, txt, own, ip, coef, gi, gt, gix, zs, zr, gtb, xr, ys, yr, gsum, gland,
    delta, g, ax, a, ap, ay, az, ag, lp, lc, lt, lx,
    hsem, fs, fr, ps, pr, isn, irc, ic_s, ic_r, ts_s, ts_r, ys_s, ys_r, xs_s, xs_r,
    gx_s, gx_r, zs_s, zs_r, xr_s, xr_r, yr_s, yr_r, gl_s, gl_r, d_s, d_r,
    ax_s, ax_r, ay_s, ay_r, az_s, az_r, ag_s, ag_r, o_s, o_r, oc_s, oc_r,
    lc_s, lc_r, lt_s, lt_r, lx_s, lx_r,
):
    x, y, zh, zl, c = place()
    z = zh * NT + zl
    other = device(x, y, z, 1 - c)
    half = y // 4

    def at_x(k):
        xx = lax.rem(x + k, NX)
        return xx, device(xx, y, z, c)

    def at_y(yy):
        return device(x, yy, z, c)

    def at_z(zz):
        return device(x, y, zz, c)

    @pl.when(c == 0)
    def _():
        pltpu.make_async_copy(hi, h, hsem).start()

    @pl.when(c == 1)
    def _():
        pltpu.make_async_copy(ht, h, hsem).start()

    barrier = pltpu.get_barrier_semaphore()

    def greet(dev):
        pl.semaphore_signal(barrier, inc=1, device_id=dev, device_id_type=MESH)

    greet(other)
    for k in range(1, NX):
        greet(at_x(k)[1])
    for k in range(1, NY):
        greet(at_y(lax.rem(y + k, NY)))
    for k in range(1, NZ):
        greet(at_z(lax.rem(z + k, NZ)))
    pl.semaphore_wait(barrier, 1 + NX - 1 + NY - 1 + NZ - 1)

    @pl.when(c == 0)
    def _():
        copy(ft, fx, fs, fr, other).start()

    @pl.when(c == 1)
    def _():
        copy(fi, fx, fs, fr, other).start()

    copy(ft, fx, fs, fr, other).wait()

    def gather_features(first, second):
        fst = first[...].astype(F32)
        snd = second[...].astype(F32)
        for t in range(NT):
            fa[t * U : (t + 1) * U, :] = jnp.concatenate(
                [fst[24 * t : 24 * t + 24], snd[24 * t : 24 * t + 24]], axis=0
            ).astype(BF16)

    @pl.when(c == 0)
    def _():
        gather_features(fi, fx)

    @pl.when(c == 1)
    def _():
        gather_features(fx, ft)

    pltpu.make_async_copy(hi, h, hsem).wait()

    part[...] = jnp.dot(fa[...], h[...], preferred_element_type=F32)
    spart[...] = part[...].astype(BF16)

    def part_copy(to):
        return copy(
            spart.at[rows(to)], rpart.at[rows(zl)], ps.at[to], pr.at[zl], at_z(zh * NT + to)
        )

    def part_wait(src):
        copy(spart.at[rows(0)], rpart.at[rows(src)], ps.at[0], pr.at[src], other).wait_recv()

    for k in range(1, NT):
        part_copy(lax.rem(zl + k, NT)).start()
    raw = part[rows(zl), :]
    for k in range(1, NT):
        src = lax.rem(zl + k, NT)
        part_wait(src)
        raw = raw + rpart[rows(src), :].astype(F32)
    inverse = lax.rsqrt(jnp.sum(raw * raw, axis=-1, keepdims=True) + norm_eps)
    raw = raw * inverse
    unit[...] = raw
    inv[...] = jnp.broadcast_to(inverse, (U, 128))
    own[...] = raw.astype(BF16)

    mine = rows(lax.rem(y, 4) * NX + x)

    def img_up(slot):
        return copy(
            img.at[rows(slot)], img.at[rows(slot)], isn.at[0, slot], irc.at[slot],
            at_z(lax.rem(z + 1, NZ)),
        )

    def img_down(slot):
        return copy(
            img.at[rows(slot)], img.at[rows(slot)], isn.at[1, slot], irc.at[slot],
            at_z(lax.rem(z + NZ - 1, NZ)),
        )

    def img_over(slot):
        return copy(
            img.at[rows(slot)], img.at[rows(slot)], ic_s.at[slot], ic_r.at[slot], other
        )

    def txt_over():
        return copy(own, txt.at[mine], ts_s, ts_r, other)

    def txt_y(to):
        return copy(txt.at[mine], txt.at[mine], ys_s.at[to], ys_r.at[lax.rem(y, 4)], at_y(to))

    def txt_x(yi, k):
        xx, dev = at_x(k)
        slot = rows(yi * NX + x)
        return copy(txt.at[slot], txt.at[slot], xs_s.at[yi, xx], xs_r.at[yi, x], dev)

    def txt_y_send():
        for k in (4, 3, 5, 2, 6, 1, 7):
            txt_y(lax.rem(y + k, NY)).start()

    def txt_forward(k):
        yi = lax.rem(y + k, 4)

        @pl.when(4 * c + yi != y)
        def _():
            slot = rows(yi * NX + x)
            copy(txt.at[slot], txt.at[slot], ys_s.at[0], ys_r.at[yi], other).wait_recv()

        for kx in (2, 1, 3):
            txt_x(yi, kx).start()

    @pl.when(c == 1)
    def _():
        @pl.when(half == 0)
        def _():
            txt_over().start()

        @pl.when(half == 1)
        def _():
            txt[mine, :] = own[...]
            txt_y_send()

        for k in range(4):
            txt_forward(k)
        for s in range(NZ):
            img_over(s).wait_recv()

    @pl.when(c == 0)
    def _():
        img[rows(z), :] = own[...]
        img_up(z).start()
        img_down(z).start()
        img_over(z).start()

        @pl.when(half == 0)
        def _():
            txt_over().wait_recv()
            txt_y_send()

        for s in range(1, 7):
            lo = lax.rem(z + NZ - s, NZ)
            hi_ = lax.rem(z + s, NZ)
            img_up(lo).wait_recv()
            if s < 6:
                img_up(lo).start()
            img_over(lo).start()
            if s < 6:
                img_down(hi_).wait_recv()
                if s < 5:
                    img_down(hi_).start()
                img_over(hi_).start()
            if s <= 4:
                txt_forward(s - 1)

    for yi in range(4):
        for k in range(1, NX):
            xx = lax.rem(x + k, NX)
            slot = rows(yi * NX + xx)
            copy(txt.at[slot], txt.at[slot], xs_s.at[0, 0], xs_r.at[yi, xx], other).wait_recv()

    ip[...] = lax.dot_general(
        img[...], txt[...], (((1,), (1,)), ((), ())), preferred_element_type=F32
    )
    mult, shift = scale[0], bias[0]
    factor = mult * (1.0 / (NX * NY * NZ * U))

    def pairs(i, total):
        r = rows(i)
        logits = mult * ip[r, :] + shift
        same = ids_i[r, :] == ids_t[...]
        v = jnp.where(same, logits, -logits)
        e = jnp.exp(-jnp.abs(v))
        d = 1.0 / (1.0 + e)
        sig = jnp.where(v >= 0, e * d, d)
        coef[r, :] = (jnp.where(same, -factor, factor) * sig).astype(BF16)
        ls = jnp.log1p(e) - jnp.minimum(v, 0.0)
        ls = jnp.sum(ls.reshape(U // 8, 8, NJ), axis=0)
        for j in range(NJ // 128):
            total = total + ls[:, 128 * j : 128 * (j + 1)]
        return total

    lp[...] = lax.fori_loop(0, NZ, pairs, jnp.zeros((8, 128), F32))

    def lc_copy():
        return copy(lp, lc, lc_s, lc_r, other)

    lc_copy().start()

    def gx_copy(q, to_core):
        return copy(gi.at[rows(2 * q + to_core)], gix.at[rows(q)], gx_s.at[q], gx_r.at[q], other)

    gi[...] = jnp.dot(coef[...], txt[...], preferred_element_type=F32)
    for q in range(NZ // 2):
        gx_copy(q, 1 - c).start()

    gt[...] = lax.dot_general(
        coef[...], img[...], (((0,), (0,)), ((), ())), preferred_element_type=F32
    )

    def xr_copy(yi, k):
        xx, dev = at_x(k)
        return copy(
            gtb.at[rows(yi * NX + xx)], xr.at[rows(yi * NX + x)], xr_s.at[yi, xx], xr_r.at[yi, x],
            dev,
        )

    for k in range(4):
        yi = lax.rem(y + 1 + k, 4)
        blk = rows(yi, NX * U)
        gtb[blk, :] = gt[blk, :].astype(BF16)
        for kx in (2, 1, 3):
            xr_copy(yi, kx).start()

    def zs_copy(q):
        to = 2 * q + c
        return copy(zs.at[rows(q)], zr.at[rows(z)], zs_s.at[q], zr_r.at[z], at_z(to))

    zr_r = zs_r
    for k in range(NZ // 2):
        q = lax.rem(z // 2 + 3 + k, 6)
        gx_copy(q, c).wait_recv()
        to = 2 * q + c
        s = gi[rows(to), :] + gix[rows(q), :]
        zs[rows(q), :] = s.astype(BF16)

        @pl.when(to != z)
        def _():
            zs_copy(q).start()

        @pl.when(to == z)
        def _():
            gsum[0] = s

    def yr_copy(yi):
        to = 4 * c + yi
        return copy(ys.at[rows(yi)], yr.at[rows(y)], yr_s.at[yi], yr_r.at[y], at_y(to))

    for k in range(4):
        yi = lax.rem(y + 1 + k, 4)
        s = gt[rows(yi * NX + x), :]
        for kx in range(1, NX):
            xx = lax.rem(x + kx, NX)
            slot = rows(yi * NX + xx)
            copy(gtb.at[slot], xr.at[slot], xr_s.at[0, 0], xr_r.at[yi, xx], other).wait_recv()
            s = s + xr[slot, :].astype(F32)
        ys[rows(yi), :] = s.astype(BF16)

        @pl.when(4 * c + yi != y)
        def _():
            yr_copy(yi).start()

        @pl.when(4 * c + yi == y)
        def _():
            gsum[1] = s

    def gl_copy(m):
        return copy(gsum.at[m], gland, gl_s, gl_r, other)

    @pl.when(lax.rem(z, 2) == c)
    def _():
        s = gsum[0]
        for k in range(1, NZ):
            src = lax.rem(z + k, NZ)
            copy(zs.at[rows(0)], zr.at[rows(src)], zs_s.at[0], zr_r.at[src], other).wait_recv()
            s = s + zr[rows(src), :].astype(F32)
        gsum[0] = s

        @pl.when(c == 1)
        def _():
            gl_copy(0).start()

    @pl.when(half == c)
    def _():
        s = gsum[1]
        for k in range(1, NY):
            src = lax.rem(y + k, NY)
            copy(ys.at[rows(0)], yr.at[rows(src)], yr_s.at[0], yr_r.at[src], other).wait_recv()
            s = s + yr[rows(src), :].astype(F32)
        gsum[1] = s

        @pl.when(c == 0)
        def _():
            gl_copy(1).start()

    @pl.when(jnp.logical_and(c == 0, lax.rem(z, 2) == 1))
    def _():
        gl_copy(0).wait_recv()
        gsum[0] = gland[...]

    @pl.when(jnp.logical_and(c == 1, half == 0))
    def _():
        gl_copy(0).wait_recv()
        gsum[1] = gland[...]

    grad = gsum[c]
    un = unit[...]
    dl = inv[:, 0:1] * (grad - un * jnp.sum(un * grad, axis=-1, keepdims=True))
    delta[rows(zl), :] = dl.astype(BF16)

    lc_copy().wait_recv()
    lt[rows(zl, 8), :] = lp[...] + lc[...]

    def d_copy(to):
        return copy(
            delta.at[rows(zl)], delta.at[rows(zl)], d_s.at[to], d_r.at[zl], at_z(zh * NT + to)
        )

    def lt_copy(to):
        return copy(
            lt.at[rows(zl, 8)], lt.at[rows(zl, 8)], lt_s.at[to], lt_r.at[zl], at_z(zh * NT + to)
        )

    for k in range(1, NT):
        to = lax.rem(zl + k, NT)
        d_copy(to).start()
        lt_copy(to).start()
    for k in range(1, NT):
        src = lax.rem(zl + k, NT)
        copy(delta.at[rows(0)], delta.at[rows(src)], d_s.at[0], d_r.at[src], other).wait_recv()
        copy(lt.at[rows(0, 8)], lt.at[rows(src, 8)], lt_s.at[0], lt_r.at[src], other).wait_recv()
    ls = lt[0:8, :]
    for t in range(1, NT):
        ls = ls + lt[8 * t : 8 * t + 8, :]
    lx[rows(x, 8), :] = ls

    g[...] = lax.dot_general(
        fa[...], delta[...], (((0,), (0,)), ((), ())), preferred_element_type=F32
    )

    def ax_copy(k):
        xx, dev = at_x(k)
        return copy(g.at[rows(xx)], ax.at[rows(x)], ax_s.at[xx], ax_r.at[x], dev)

    def lx_copy(k):
        xx, dev = at_x(k)
        return copy(lx.at[rows(x, 8)], lx.at[rows(x, 8)], lx_s.at[xx], lx_r.at[x], dev)

    for k in (2, 1, 3):
        ax_copy(k).start()
        lx_copy(k).start()
    s = g[rows(x), :]
    for k in range(1, NX):
        xx = lax.rem(x + k, NX)
        copy(g.at[rows(0)], ax.at[rows(xx)], ax_s.at[0], ax_r.at[xx], other).wait_recv()
        s = s + ax[rows(xx), :]
        copy(lx.at[rows(0, 8)], lx.at[rows(xx, 8)], lx_s.at[0], lx_r.at[xx], other).wait_recv()
    for k in range(NY):
        ap[k, 0:U, :] = s[:, 128 * k : 128 * (k + 1)]
    for k in range(6):
        ap[k, U : U + 8, :] = s[8 * k : 8 * k + 8, 1024:1152]
    ls = lx[0:8, :]
    for t in range(1, NX):
        ls = ls + lx[8 * t : 8 * t + 8, :]
    ap[6, U : U + 8, :] = ls
    ap[7, U : U + 8, :] = ls

    def ay_copy(to):
        return copy(ap.at[to], ay.at[y], ay_s.at[to], ay_r.at[y], at_y(to))

    for k in (4, 3, 5, 2, 6, 1, 7):
        ay_copy(lax.rem(y + k, NY)).start()
    s = ap[y]
    for k in range(1, NY):
        src = lax.rem(y + k, NY)
        copy(ap.at[0], ay.at[src], ay_s.at[0], ay_r.at[src], other).wait_recv()
        s = s + ay[src]
    a[...] = s
    az_copy = copy(a, az, az_s, az_r, at_z(lax.rem(z + NT, NZ)))
    az_copy.start()
    az_copy.wait()
    ag[y] = s + az[...]

    def ag_copy(to):
        return copy(ag.at[y], ag.at[y], ag_s.at[to], ag_r.at[y], at_y(to))

    for k in (4, 3, 5, 2, 6, 1, 7):
        ag_copy(lax.rem(y + k, NY)).start()
    for k in range(1, NY):
        src = lax.rem(y + k, NY)
        copy(ag.at[0], ag.at[src], ag_s.at[0], ag_r.at[src], other).wait_recv()
    for k in range(NY):
        out[c, rows(x), 128 * k : 128 * (k + 1)] = ag[k, 0:U, :]
    for k in range(6):
        out[c, pl.ds(pl.multiple_of(x * U + 8 * k, 8), 8), 1024:1152] = ag[k, U : U + 8, :]

    def o_copy(k):
        xx, dev = at_x(k)
        blk = out.at[c, rows(x)]
        return copy(blk, blk, o_s.at[xx], o_r.at[x], dev)

    def oc_copy(xx, m):
        blk = out.at[m, rows(xx)]
        return copy(blk, blk, oc_s.at[xx], oc_r.at[xx], other)

    for k in (2, 1, 3):
        o_copy(k).start()
    oc_copy(x, c).start()
    for k in range(1, NX):
        xx = lax.rem(x + k, NX)
        blk = out.at[c, rows(xx)]
        copy(blk, blk, o_s.at[0], o_r.at[xx], other).wait_recv()
        oc_copy(xx, c).start()
    loss_out[...] = jnp.broadcast_to(
        jnp.sum(ag[6, U : U + 8, :], keepdims=True) * (1.0 / (NX * NY * NZ * U)), (8, 128)
    )
    for xx in range(NX):
        oc_copy(xx, 1 - c).wait_recv()

    for k in range(1, NT):
        to = lax.rem(zl + k, NT)
        part_copy(to).wait_send()
        d_copy(to).wait_send()
        lt_copy(to).wait_send()

    @pl.when(c == 0)
    def _():
        img_up(z).wait_send()
        img_down(z).wait_send()
        for s in range(1, 6):
            img_up(lax.rem(z + NZ - s, NZ)).wait_send()
            if s < 5:
                img_down(lax.rem(z + s, NZ)).wait_send()
        for s in range(NZ):
            img_over(s).wait_send()

    @pl.when(jnp.logical_and(c == 1, half == 0))
    def _():
        txt_over().wait_send()

    @pl.when(half == c)
    def _():
        for k in range(1, NY):
            txt_y(lax.rem(y + k, NY)).wait_send()

    for yi in range(4):
        for k in range(1, NX):
            txt_x(yi, k).wait_send()
            xr_copy(yi, k).wait_send()

        @pl.when(4 * c + yi != y)
        def _():
            yr_copy(yi).wait_send()

    lc_copy().wait_send()
    for q in range(NZ // 2):
        gx_copy(q, 1 - c).wait_send()

        @pl.when(2 * q + c != z)
        def _():
            zs_copy(q).wait_send()

    @pl.when(jnp.logical_and(c == 1, lax.rem(z, 2) == 1))
    def _():
        gl_copy(0).wait_send()

    @pl.when(jnp.logical_and(c == 0, half == 0))
    def _():
        gl_copy(1).wait_send()

    for k in range(1, NX):
        ax_copy(k).wait_send()
        lx_copy(k).wait_send()
        o_copy(k).wait_send()
    for k in range(1, NY):
        to = lax.rem(y + k, NY)
        ay_copy(to).wait_send()
        ag_copy(to).wait_send()
    for xx in range(NX):
        oc_copy(xx, c).wait_send()


def on_device(
    image_features, text_features, image_head, text_head, caption_ids, logit_scale, logit_bias
):
    x, y, zh, zl, c = place()
    table = caption_ids.reshape(NY, NX, 2, 2, NT, 24)
    ids_i = lax.dynamic_slice(table, (y, x, 0, 0, 0, 0), (1, 1, 2, 2, NT, 24))
    ids_i = ids_i.reshape(2, 2, NT, 24).transpose(0, 2, 1, 3).reshape(NI, 1)
    ids_t = lax.dynamic_slice(table, (4 * c, 0, zh, 0, zl, 0), (4, NX, 1, 2, 1, 24)).reshape(1, NJ)
    vm = pl.BlockSpec(memory_space=pltpu.VMEM)
    sm = pl.BlockSpec(memory_space=pltpu.SMEM)
    dma = pltpu.SemaphoreType.DMA
    scratch = dict(
        h=((192, E), BF16), fx=((144, 192), BF16), fa=((NT * U, 192), BF16),
        part=((NT * U, E), F32), spart=((NT * U, E), BF16), rpart=((NT * U, E), BF16),
        unit=((U, E), F32), inv=((U, 128), F32),
        img=((NI, E), BF16), txt=((NJ, E), BF16), own=((U, E), BF16),
        ip=((NI, NJ), F32), coef=((NI, NJ), BF16), gi=((NI, E), F32), gt=((NJ, E), F32),
        gix=((NI // 2, E), F32), zs=((NI // 2, E), BF16), zr=((NI, E), BF16),
        gtb=((NJ, E), BF16), xr=((NJ, E), BF16), ys=((4 * U, E), BF16), yr=((NY * U, E), BF16),
        gsum=((2, U, E), F32), gland=((U, E), F32),
        delta=((NT * U, E), BF16), g=((192, E), F32), ax=((192, E), F32),
        a=((U + 8, 128), F32), ap=((NY, U + 8, 128), F32), ay=((NY, U + 8, 128), F32),
        az=((U + 8, 128), F32), ag=((NY, U + 8, 128), F32),
        lp=((8, 128), F32), lc=((8, 128), F32), lt=((8 * NT, 128), F32), lx=((8 * NX, 128), F32),
    )
    sems = [
        (), (), (), (NT,), (NT,), (2, NZ), (NZ,), (NZ,), (NZ,), (), (), (NY,), (4,), (4, NX), (4, NX),
        (6,), (6,), (6,), (NZ,), (4, NX), (4, NX), (4,), (NY,), (), (), (NT,), (NT,),
        (NX,), (NX,), (NY,), (NY,), (), (), (NY,), (NY,), (NX,), (NX,), (NX,), (NX,),
        (), (), (NT,), (NT,), (NX,), (NX,),
    ]
    out, loss = pl.pallas_call(
        kernel,
        out_shape=(
            jax.ShapeDtypeStruct((2, 192, E), F32),
            jax.ShapeDtypeStruct((8, 128), F32),
        ),
        in_specs=[
            vm, vm, pl.BlockSpec(memory_space=pl.ANY), pl.BlockSpec(memory_space=pl.ANY),
            vm, vm, sm, sm,
        ],
        out_specs=(vm, vm),
        scratch_shapes=[pltpu.VMEM(*scratch[n]) for n in scratch]
        + [dma(s) if s else dma for s in sems],
        compiler_params=pltpu.CompilerParams(
            collective_id=0, has_side_effects=True, vmem_limit_bytes=56 * 2**20
        ),
        cost_estimate=pl.CostEstimate(
            flops=4 * 10**9, bytes_accessed=10**7, transcendentals=10**6
        ),
        name="siglip",
    )(
        image_features, text_features, image_head, text_head, ids_i, ids_t, logit_scale, logit_bias
    )
    return loss[0, :1], out[0], out[1]


def solution(mesh):
    placed = (
        P("batch", "tower"),
        P("batch", "tower"),
        P("tower", None),
        P("tower", None),
        P(),
        P(),
        P(),
    )
    return jax.shard_map(
        on_device,
        mesh=mesh,
        in_specs=placed,
        out_specs=(P(), P("tower", None), P("tower", None)),
        check_vma=False,
    )
```

time: 2430 us -> 182 us (0.07)
  waiting for transfers between devices: 1870 us -> 0 us
  blocking collectives: 502 us -> 0 us
  Pallas kernels: 0 us -> 172 us
  matrix products: 25.8 us -> 0 us
    psum x3 -> x0, waiting for transfers between devices: 1530 us -> none  [the longest x1 1330 us: on_device(): lax.psum((image_head_part, text_head_part, group_loss), 'batch')]
    psum x2 -> x0, blocking collectives: 502 us -> none  [the longest x1 485 us: on_device(): lax.psum((image_head_part, text_head_part, group_loss), 'batch')]
    all_gather x2 -> x0, waiting for transfers between devices: 346 us -> none  [the longest x1 180 us: on_device(): lax.all_gather(text_share, 'batch', axis=0, tiled=True)]
    pallas_call x0 -> x1, Pallas kernels: none -> 172 us  [on_device(): pl.pallas_call(kernel, out_shape=(jax.ShapeDtypeStruct((2, 192, E), F32),...]
    dot_general x7 -> x0, matrix products: 25.8 us -> none  [the longest x3 12.2 us: transpose_product(): lax.dot_general(left, right, (((0,), (0,)), ((), ())), preferred_element_...]
  transfers between devices with their start and end apart: 5 -> 0, of which waited for: 5 -> 0; matrix products, arithmetic and copies ran while one was open for 0% -> 0% of each run, Pallas kernels for 0% -> 0%
where the time goes in v1:
time: 182 us; the launch traced here: 181 us
  Pallas kernels  172 us (95%)
  local copies, waits for them, and re-layouts  6.7 us (4%)
  between operations  2.02 us (1%)
    pallas_call x1, Pallas kernels, on_device(): pl.pallas_call(kernel, out_shape=(jax.ShapeDtypeStruct((2, 192, E), F32),...  172 us

profile of v1, /device:TPU:1, one launch (start us, length us, event | category | flops | bytes accessed | tf_op | source)
XLA Modules:
  0.0 180.6 jit_solution(15509664234132475606)
XLA Ops:
  2.0 1.1 reshape.18
  3.1 0.1 dynamic-slice_reduce_fusion
  3.2 0.7 reshape.21.ids_t
  3.9 0.9 reshape.22.ids_i
  4.8 171.9 %siglip.1 = (f32[2,192,1152]{2,1,0:T(8,128)}, f32[8,128]{1,0:T(8,128)}) custom-call(bf16[144,192]{1,0:T(8,128)(2,1)} %fi.1, bf16[144,192]{1,0:T(8,128)(2,1)} %ft.1, bf16[192,1152]{1,0:T(8,128)(2,1)} %hi.1, bf16[192,1152]{1,0:T(8,128)(2,1)} %ht.1, s32[576,1]{1,0:T(8,128)} %reshape.22.ids_i, s32[1,768]{1,0:T(1,128)} %reshape.21.ids_t, f32[1]{0:T(128)S(6)} %copy.15.scale, ...), custom_call_target="tpu_custom_call" | custom-call | flops 4000000000 | bytes 10000000 | tf_op jit(solution)/shard_map/siglip/pallas_call | solution.py:579
  176.7 1.2 slice.9
  177.9 2.8 %slice_bitcast_fusion = (f32[192,1152]{1,0:T(8,128)}, f32[192,1152]{1,0:T(8,128)}) fusion(f32[2,192,1152]{2,1,0:T(8,128)} %get-tuple-element.6), kind=kLoop, calls=%fused_computation | loop fusion | bytes 3538944 | tf_op jit(solution)/shard_map/squeeze | solution.py:602
  (2 shorter events, 0.0 us)

commit v2 on v1

--- a/solution.py
+++ b/solution.py
@@ -12,6 +12,7 @@
 NX, NY, NZ, NT = 4, 8, 12, 6
 E = 1152
 U = 48
+NP = 3
 NI, NJ = NZ * U, 4 * NX * U
 norm_eps = 1e-06
 
@@ -42,10 +43,10 @@
 
 def kernel(
     fi, ft, hi, ht, ids_i, ids_t, scale, bias,
-    out, loss_out,
+    out_i, out_t, loss_out,
     h, fx, fa, part, spart, rpart, unit, inv,
     img, txt, own, ip, coef, gi, gt, gix, zs, zr, gtb, xr, ys, yr, gsum, gland,
-    delta, g, ax, a, ap, ay, az, ag, lp, lc, lt, lx,
+    delta, g, gb, ax, ob, a, ap, ay, az, ag, lp, lc, lt, lx,
     hsem, fs, fr, ps, pr, isn, irc, ic_s, ic_r, ts_s, ts_r, ys_s, ys_r, xs_s, xs_r,
     gx_s, gx_r, zs_s, zs_r, xr_s, xr_r, yr_s, yr_r, gl_s, gl_r, d_s, d_r,
     ax_s, ax_r, ay_s, ay_r, az_s, az_r, ag_s, ag_r, o_s, o_r, oc_s, oc_r,
@@ -115,6 +116,9 @@
         gather_features(fx, ft)
 
     pltpu.make_async_copy(hi, h, hsem).wait()
+
+    def piece(d, p):
+        return rows(d * NP + p, U // NP)
 
     part[...] = jnp.dot(fa[...], h[...], preferred_element_type=F32)
     spart[...] = part[...].astype(BF16)
@@ -265,14 +269,6 @@
     def gx_copy(q, to_core):
         return copy(gi.at[rows(2 * q + to_core)], gix.at[rows(q)], gx_s.at[q], gx_r.at[q], other)
 
-    gi[...] = jnp.dot(coef[...], txt[...], preferred_element_type=F32)
-    for q in range(NZ // 2):
-        gx_copy(q, 1 - c).start()
-
-    gt[...] = lax.dot_general(
-        coef[...], img[...], (((0,), (0,)), ((), ())), preferred_element_type=F32
-    )
-
     def xr_copy(yi, k):
         xx, dev = at_x(k)
         return copy(
@@ -280,12 +276,32 @@
             dev,
         )
 
-    for k in range(4):
-        yi = lax.rem(y + 1 + k, 4)
-        blk = rows(yi, NX * U)
+    for jb in range(2):
+        blk = slice(jb * NJ // 2, (jb + 1) * NJ // 2)
+        gt[blk, :] = lax.dot_general(
+            coef[:, blk], img[...], (((0,), (0,)), ((), ())), preferred_element_type=F32
+        )
         gtb[blk, :] = gt[blk, :].astype(BF16)
-        for kx in (2, 1, 3):
-            xr_copy(yi, kx).start()
+        for yi in (2 * jb, 2 * jb + 1):
+            for kx in (2, 1, 3):
+                xr_copy(yi, kx).start()
+
+    for ib in range(3):
+        blk = slice(ib * NI // 3, (ib + 1) * NI // 3)
+        gi[blk, :] = jnp.dot(coef[blk, :], txt[...], preferred_element_type=F32)
+        for q in (2 * ib, 2 * ib + 1):
+            gx_copy(q, 1 - c).start()
+
+    lc_copy().wait_recv()
+    lt[rows(zl, 8), :] = lp[...] + lc[...]
+
+    def lt_copy(to):
+        return copy(
+            lt.at[rows(zl, 8)], lt.at[rows(zl, 8)], lt_s.at[to], lt_r.at[zl], at_z(zh * NT + to)
+        )
+
+    for k in range(1, NT):
+        lt_copy(lax.rem(zl + k, NT)).start()
 
     def zs_copy(q):
         to = 2 * q + c
@@ -293,7 +309,7 @@
 
     zr_r = zs_r
     for k in range(NZ // 2):
-        q = lax.rem(z // 2 + 3 + k, 6)
+        q = k
         gx_copy(q, c).wait_recv()
         to = 2 * q + c
         s = gi[rows(to), :] + gix[rows(q), :]
@@ -311,8 +327,7 @@
         to = 4 * c + yi
         return copy(ys.at[rows(yi)], yr.at[rows(y)], yr_s.at[yi], yr_r.at[y], at_y(to))
 
-    for k in range(4):
-        yi = lax.rem(y + 1 + k, 4)
+    for yi in range(4):
         s = gt[rows(yi * NX + x), :]
         for kx in range(1, NX):
             xx = lax.rem(x + kx, NX)
@@ -373,26 +388,38 @@
     dl = inv[:, 0:1] * (grad - un * jnp.sum(un * grad, axis=-1, keepdims=True))
     delta[rows(zl), :] = dl.astype(BF16)
 
-    lc_copy().wait_recv()
-    lt[rows(zl, 8), :] = lp[...] + lc[...]
-
-    def d_copy(to):
-        return copy(
-            delta.at[rows(zl)], delta.at[rows(zl)], d_s.at[to], d_r.at[zl], at_z(zh * NT + to)
-        )
-
-    def lt_copy(to):
-        return copy(
-            lt.at[rows(zl, 8)], lt.at[rows(zl, 8)], lt_s.at[to], lt_r.at[zl], at_z(zh * NT + to)
-        )
-
+    def d_copy(src, p, right):
+        blk = piece(src, p)
+        i = src * NP + p
+        dev = at_z(lax.rem(z + (1 if right else NZ - 1), NZ))
+        return copy(delta.at[blk], delta.at[blk], d_s.at[0 if right else 1, i], d_r.at[i], dev)
+
+    def d_step(src, p, right):
+        @pl.when(zl != (NT - 1 if right else 0))
+        def _():
+            d_copy(src, p, right).start()
+
+    def d_wait(src, p):
+        d_copy(src, p, True).wait_recv()
+
+    for p in range(NP):
+        d_step(zl, p, True)
+        d_step(zl, p, False)
     for k in range(1, NT):
-        to = lax.rem(zl + k, NT)
-        d_copy(to).start()
-        lt_copy(to).start()
+        for p in range(NP):
+
+            @pl.when(zl >= k)
+            def _():
+                d_wait(zl - k, p)
+                d_step(zl - k, p, True)
+
+            @pl.when(zl + k < NT)
+            def _():
+                d_wait(zl + k, p)
+                d_step(zl + k, p, False)
+
     for k in range(1, NT):
         src = lax.rem(zl + k, NT)
-        copy(delta.at[rows(0)], delta.at[rows(src)], d_s.at[0], d_r.at[src], other).wait_recv()
         copy(lt.at[rows(0, 8)], lt.at[rows(src, 8)], lt_s.at[0], lt_r.at[src], other).wait_recv()
     ls = lt[0:8, :]
     for t in range(1, NT):
@@ -403,9 +430,11 @@
         fa[...], delta[...], (((0,), (0,)), ((), ())), preferred_element_type=F32
     )
 
+    gb[...] = g[...].astype(BF16)
+
     def ax_copy(k):
         xx, dev = at_x(k)
-        return copy(g.at[rows(xx)], ax.at[rows(x)], ax_s.at[xx], ax_r.at[x], dev)
+        return copy(gb.at[rows(xx)], ax.at[rows(x)], ax_s.at[xx], ax_r.at[x], dev)
 
     def lx_copy(k):
         xx, dev = at_x(k)
@@ -417,8 +446,8 @@
     s = g[rows(x), :]
     for k in range(1, NX):
         xx = lax.rem(x + k, NX)
-        copy(g.at[rows(0)], ax.at[rows(xx)], ax_s.at[0], ax_r.at[xx], other).wait_recv()
-        s = s + ax[rows(xx), :]
+        copy(gb.at[rows(0)], ax.at[rows(xx)], ax_s.at[0], ax_r.at[xx], other).wait_recv()
+        s = s + ax[rows(xx), :].astype(F32)
         copy(lx.at[rows(0, 8)], lx.at[rows(xx, 8)], lx_s.at[0], lx_r.at[xx], other).wait_recv()
     for k in range(NY):
         ap[k, 0:U, :] = s[:, 128 * k : 128 * (k + 1)]
@@ -454,18 +483,18 @@
     for k in range(1, NY):
         src = lax.rem(y + k, NY)
         copy(ag.at[0], ag.at[src], ag_s.at[0], ag_r.at[src], other).wait_recv()
-    for k in range(NY):
-        out[c, rows(x), 128 * k : 128 * (k + 1)] = ag[k, 0:U, :]
-    for k in range(6):
-        out[c, pl.ds(pl.multiple_of(x * U + 8 * k, 8), 8), 1024:1152] = ag[k, U : U + 8, :]
+    last = jnp.concatenate([ag[k, U : U + 8, :] for k in range(6)], axis=0)
+    ob[c, rows(x), :] = jnp.concatenate(
+        [ag[k, 0:U, :] for k in range(NY)] + [last], axis=1
+    ).astype(BF16)
 
     def o_copy(k):
         xx, dev = at_x(k)
-        blk = out.at[c, rows(x)]
+        blk = ob.at[c, rows(x)]
         return copy(blk, blk, o_s.at[xx], o_r.at[x], dev)
 
     def oc_copy(xx, m):
-        blk = out.at[m, rows(xx)]
+        blk = ob.at[m, rows(xx)]
         return copy(blk, blk, oc_s.at[xx], oc_r.at[xx], other)
 
     for k in (2, 1, 3):
@@ -473,20 +502,29 @@
     oc_copy(x, c).start()
     for k in range(1, NX):
         xx = lax.rem(x + k, NX)
-        blk = out.at[c, rows(xx)]
+        blk = ob.at[c, rows(xx)]
         copy(blk, blk, o_s.at[0], o_r.at[xx], other).wait_recv()
         oc_copy(xx, c).start()
-    loss_out[...] = jnp.broadcast_to(
-        jnp.sum(ag[6, U : U + 8, :], keepdims=True) * (1.0 / (NX * NY * NZ * U)), (8, 128)
-    )
+    loss_out[0] = jnp.sum(ag[6, U : U + 8, :]) * (1.0 / (NX * NY * NZ * U))
     for xx in range(NX):
         oc_copy(xx, 1 - c).wait_recv()
+    out_i[...] = ob[0].astype(F32)
+    out_t[...] = ob[1].astype(F32)
 
     for k in range(1, NT):
         to = lax.rem(zl + k, NT)
         part_copy(to).wait_send()
-        d_copy(to).wait_send()
         lt_copy(to).wait_send()
+    for d in range(NT):
+        for p in range(NP):
+
+            @pl.when(jnp.logical_and(d <= zl, zl != NT - 1))
+            def _():
+                d_copy(d, p, True).wait_send()
+
+            @pl.when(jnp.logical_and(d >= zl, zl != 0))
+            def _():
+                d_copy(d, p, False).wait_send()
 
     @pl.when(c == 0)
     def _():
@@ -565,28 +603,30 @@
         gix=((NI // 2, E), F32), zs=((NI // 2, E), BF16), zr=((NI, E), BF16),
         gtb=((NJ, E), BF16), xr=((NJ, E), BF16), ys=((4 * U, E), BF16), yr=((NY * U, E), BF16),
         gsum=((2, U, E), F32), gland=((U, E), F32),
-        delta=((NT * U, E), BF16), g=((192, E), F32), ax=((192, E), F32),
+        delta=((NT * U, E), BF16), g=((192, E), F32), gb=((192, E), BF16), ax=((192, E), BF16),
+        ob=((2, 192, E), BF16),
         a=((U + 8, 128), F32), ap=((NY, U + 8, 128), F32), ay=((NY, U + 8, 128), F32),
         az=((U + 8, 128), F32), ag=((NY, U + 8, 128), F32),
         lp=((8, 128), F32), lc=((8, 128), F32), lt=((8 * NT, 128), F32), lx=((8 * NX, 128), F32),
     )
     sems = [
         (), (), (), (NT,), (NT,), (2, NZ), (NZ,), (NZ,), (NZ,), (), (), (NY,), (4,), (4, NX), (4, NX),
-        (6,), (6,), (6,), (NZ,), (4, NX), (4, NX), (4,), (NY,), (), (), (NT,), (NT,),
+        (6,), (6,), (6,), (NZ,), (4, NX), (4, NX), (4,), (NY,), (), (), (2, NT * NP), (NT * NP,),
         (NX,), (NX,), (NY,), (NY,), (), (), (NY,), (NY,), (NX,), (NX,), (NX,), (NX,),
         (), (), (NT,), (NT,), (NX,), (NX,),
     ]
-    out, loss = pl.pallas_call(
+    out_i, out_t, loss = pl.pallas_call(
         kernel,
         out_shape=(
-            jax.ShapeDtypeStruct((2, 192, E), F32),
-            jax.ShapeDtypeStruct((8, 128), F32),
+            jax.ShapeDtypeStruct((192, E), F32),
+            jax.ShapeDtypeStruct((192, E), F32),
+            jax.ShapeDtypeStruct((1,), F32),
         ),
         in_specs=[
             vm, vm, pl.BlockSpec(memory_space=pl.ANY), pl.BlockSpec(memory_space=pl.ANY),
             vm, vm, sm, sm,
         ],
-        out_specs=(vm, vm),
+        out_specs=(vm, vm, sm),
         scratch_shapes=[pltpu.VMEM(*scratch[n]) for n in scratch]
         + [dma(s) if s else dma for s in sems],
         compiler_params=pltpu.CompilerParams(
@@ -599,7 +639,7 @@
     )(
         image_features, text_features, image_head, text_head, ids_i, ids_t, logit_scale, logit_bias
     )
-    return loss[0, :1], out[0], out[1]
+    return loss, out_i, out_t
 
 
 def solution(mesh):

time: 182 us -> 169 us (0.929)
  Pallas kernels: 172 us -> 160 us
    pallas_call x1, Pallas kernels: 172 us -> 160 us  [on_device(): pl.pallas_call(kernel, out_shape=(jax.ShapeDtypeStruct((192, E), F32), ja...]
    unnamed x0 -> x6, local copies, waits for them, and re-layouts: none -> 3.13 us
    squeeze x1 -> x0, local copies, waits for them, and re-layouts: 2.75 us -> none  [on_device(): return (loss[0, :1], out[0], out[1])]
where the time goes in v2:
time: 169 us; the launch traced here: 168 us
  Pallas kernels  160 us (95%)
  local copies, waits for them, and re-layouts  5.01 us (3%)
  between operations  3.78 us (2%)
    pallas_call x1, Pallas kernels, on_device(): pl.pallas_call(kernel, out_shape=(jax.ShapeDtypeStruct((192, E), F32), ja...  160 us

profile of v2, /device:TPU:1, one launch (start us, length us, event | category | flops | bytes accessed | tf_op | source)
XLA Modules:
  0.0 168.4 jit_solution(6560323911263077571)
XLA Ops:
  0.6 0.0 copy-start.1
  2.0 0.0 copy-done.1
  2.0 0.2 reshape.18
  2.3 0.1 dynamic-slice_reduce_fusion
  2.4 0.7 reshape.21.ids_t
  3.0 0.9 reshape.22.ids_i
  3.9 159.6 %siglip.1 = (f32[192,1152]{1,0:T(8,128)}, f32[192,1152]{1,0:T(8,128)}, f32[1]{0:T(128)}) custom-call(bf16[144,192]{1,0:T(8,128)(2,1)} %fi.1, bf16[144,192]{1,0:T(8,128)(2,1)} %ft.1, bf16[192,1152]{1,0:T(8,128)(2,1)} %hi.1, bf16[192,1152]{1,0:T(8,128)(2,1)} %ht.1, s32[576,1]{1,0:T(8,128)} %reshape.22.ids_i, s32[1,768]{1,0:T(1,128)} %reshape.21.ids_t, ...), custom_call_target="tpu_custom_call" | custom-call | flops 4000000000 | bytes 10000000 | tf_op jit(solution)/shard_map/siglip/pallas_call | solution.py:618
  164.1 0.0 copy-start
  164.2 2.2 %copy.21 = f32[192,1152]{1,0:T(8,128)} copy(f32[192,1152]{1,0:T(8,128)} %get-tuple-element.13) | data formatting | bytes 1769472
  166.4 0.0 copy-done
  166.4 0.9 copy.22
  (2 shorter events, 0.0 us)
Async XLA Ops:
  0.6 1.4 copy-start.1
  164.1 2.2 %copy-start = (f32[192,1152]{1,0:T(8,128)S(1)}, f32[192,1152]{1,0:T(8,128)}, u32[]{:S(2)}) copy-start(f32[192,1152]{1,0:T(8,128)} %get-tuple-element.14) | copy-start | bytes 2654212

commit v3 on v2

--- a/solution.py
+++ b/solution.py
@@ -43,10 +43,10 @@
 
 def kernel(
     fi, ft, hi, ht, ids_i, ids_t, scale, bias,
-    out_i, out_t, loss_out,
+    ob, loss_out,
     h, fx, fa, part, spart, rpart, unit, inv,
     img, txt, own, ip, coef, gi, gt, gix, zs, zr, gtb, xr, ys, yr, gsum, gland,
-    delta, g, gb, ax, ob, a, ap, ay, az, ag, lp, lc, lt, lx,
+    delta, g, gb, ax, a, ap, ay, az, ag, lp, lc, lt, lx,
     hsem, fs, fr, ps, pr, isn, irc, ic_s, ic_r, ts_s, ts_r, ys_s, ys_r, xs_s, xs_r,
     gx_s, gx_r, zs_s, zs_r, xr_s, xr_r, yr_s, yr_r, gl_s, gl_r, d_s, d_r,
     ax_s, ax_r, ay_s, ay_r, az_s, az_r, ag_s, ag_r, o_s, o_r, oc_s, oc_r,
@@ -508,8 +508,6 @@
     loss_out[0] = jnp.sum(ag[6, U : U + 8, :]) * (1.0 / (NX * NY * NZ * U))
     for xx in range(NX):
         oc_copy(xx, 1 - c).wait_recv()
-    out_i[...] = ob[0].astype(F32)
-    out_t[...] = ob[1].astype(F32)
 
     for k in range(1, NT):
         to = lax.rem(zl + k, NT)
@@ -604,7 +602,6 @@
         gtb=((NJ, E), BF16), xr=((NJ, E), BF16), ys=((4 * U, E), BF16), yr=((NY * U, E), BF16),
         gsum=((2, U, E), F32), gland=((U, E), F32),
         delta=((NT * U, E), BF16), g=((192, E), F32), gb=((192, E), BF16), ax=((192, E), BF16),
-        ob=((2, 192, E), BF16),
         a=((U + 8, 128), F32), ap=((NY, U + 8, 128), F32), ay=((NY, U + 8, 128), F32),
         az=((U + 8, 128), F32), ag=((NY, U + 8, 128), F32),
         lp=((8, 128), F32), lc=((8, 128), F32), lt=((8 * NT, 128), F32), lx=((8 * NX, 128), F32),
@@ -615,18 +612,17 @@
         (NX,), (NX,), (NY,), (NY,), (), (), (NY,), (NY,), (NX,), (NX,), (NX,), (NX,),
         (), (), (NT,), (NT,), (NX,), (NX,),
     ]
-    out_i, out_t, loss = pl.pallas_call(
+    heads, loss = pl.pallas_call(
         kernel,
         out_shape=(
-            jax.ShapeDtypeStruct((192, E), F32),
-            jax.ShapeDtypeStruct((192, E), F32),
+            jax.ShapeDtypeStruct((2, 192, E), BF16),
             jax.ShapeDtypeStruct((1,), F32),
         ),
         in_specs=[
             vm, vm, pl.BlockSpec(memory_space=pl.ANY), pl.BlockSpec(memory_space=pl.ANY),
             vm, vm, sm, sm,
         ],
-        out_specs=(vm, vm, sm),
+        out_specs=(vm, sm),
         scratch_shapes=[pltpu.VMEM(*scratch[n]) for n in scratch]
         + [dma(s) if s else dma for s in sems],
         compiler_params=pltpu.CompilerParams(
@@ -639,7 +635,7 @@
     )(
         image_features, text_features, image_head, text_head, ids_i, ids_t, logit_scale, logit_bias
     )
-    return loss, out_i, out_t
+    return loss, heads[0].astype(F32), heads[1].astype(F32)
 
 
 def solution(mesh):

time: 169 us -> 167 us (0.988)
  local copies, waits for them, and re-layouts: 5.01 us -> 1.88 us
  other arithmetic: 0 us -> 2.47 us
    unnamed x6 -> x2, local copies, waits for them, and re-layouts: 3.13 us -> 0.01 us
    convert_element_type x0 -> x1, other arithmetic: none -> 2.47 us  [on_device(): return (loss, heads[0].astype(F32), heads[1].astype(F32))]
where the time goes in v3:
time: 167 us
  Pallas kernels  159 us (95%)
  between operations  3.84 us (2%)
  other arithmetic  2.47 us (1%)
  local copies, waits for them, and re-layouts  1.88 us (1%)
    pallas_call x1, Pallas kernels, on_device(): pl.pallas_call(kernel, out_shape=(jax.ShapeDtypeStruct((2, 192, E), BF16)...  159 us

profile of v3, /device:TPU:1, one launch (start us, length us, event | category | flops | bytes accessed | tf_op | source)
XLA Modules:
  0.0 167.2 jit_solution(8715997838193981555)
XLA Ops:
  0.6 0.0 copy-start
  2.0 0.0 copy-done
  2.0 0.2 reshape.22
  2.3 0.1 dynamic-slice_reduce_fusion
  2.4 0.7 reshape.25.ids_t
  3.0 0.9 reshape.28.ids_i
  3.9 159.0 %siglip.1 = (bf16[2,192,1152]{2,1,0:T(8,128)(2,1)}, f32[1]{0:T(128)}) custom-call(bf16[144,192]{1,0:T(8,128)(2,1)} %fi.1, bf16[144,192]{1,0:T(8,128)(2,1)} %ft.1, bf16[192,1152]{1,0:T(8,128)(2,1)} %hi.1, bf16[192,1152]{1,0:T(8,128)(2,1)} %ht.1, s32[576,1]{1,0:T(8,128)} %reshape.28.ids_i, s32[1,768]{1,0:T(1,128)} %reshape.25.ids_t, f32[1]{0:T(128)S(6)} %copy.16.scale, ...), custom_call_target="tpu_custom_call" | custom-call | flops 4000000000 | bytes 10000000 | tf_op jit(solution)/shard_map/siglip/pallas_call | solution.py:615
  162.9 2.5 %bitcast_convert_fusion = (f32[192,1152]{1,0:T(8,128)}, f32[192,1152]{1,0:T(8,128)}) fusion(bf16[2,192,1152]{2,1,0:T(8,128)(2,1)} %get-tuple-element.6), kind=kLoop, calls=%fused_computation | loop fusion | flops 442368 | bytes 2654208 | tf_op jit(solution)/shard_map/convert_element_type | solution.py:638
  (2 shorter events, 0.0 us)
Async XLA Ops:
  0.6 1.4 copy-start

commit v4 on v3

--- a/solution.py
+++ b/solution.py
@@ -276,6 +276,12 @@
             dev,
         )
 
+    for ib in range(3):
+        blk = slice(ib * NI // 3, (ib + 1) * NI // 3)
+        gi[blk, :] = jnp.dot(coef[blk, :], txt[...], preferred_element_type=F32)
+        for q in (2 * ib, 2 * ib + 1):
+            gx_copy(q, 1 - c).start()
+
     for jb in range(2):
         blk = slice(jb * NJ // 2, (jb + 1) * NJ // 2)
         gt[blk, :] = lax.dot_general(
@@ -285,12 +291,6 @@
         for yi in (2 * jb, 2 * jb + 1):
             for kx in (2, 1, 3):
                 xr_copy(yi, kx).start()
-
-    for ib in range(3):
-        blk = slice(ib * NI // 3, (ib + 1) * NI // 3)
-        gi[blk, :] = jnp.dot(coef[blk, :], txt[...], preferred_element_type=F32)
-        for q in (2 * ib, 2 * ib + 1):
-            gx_copy(q, 1 - c).start()
 
     lc_copy().wait_recv()
     lt[rows(zl, 8), :] = lp[...] + lc[...]

time: 167 us -> 169 us (1.012)
  Pallas kernels: 159 us -> 161 us
where the time goes in v4:
time: 169 us
  Pallas kernels  161 us (95%)
  between operations  3.84 us (2%)
  other arithmetic  2.47 us (1%)
  local copies, waits for them, and re-layouts  1.88 us (1%)
    pallas_call x1, Pallas kernels, on_device(): pl.pallas_call(kernel, out_shape=(jax.ShapeDtypeStruct((2, 192, E), BF16)...  161 us

profile of v4, /device:TPU:1, one launch (start us, length us, event | category | flops | bytes accessed | tf_op | source)
XLA Modules:
  0.0 168.8 jit_solution(13690312091828016718)
XLA Ops:
  0.6 0.0 copy-start
  2.0 0.0 copy-done
  2.0 0.2 reshape.22
  2.3 0.1 dynamic-slice_reduce_fusion
  2.4 0.7 reshape.25.ids_t
  3.0 0.9 reshape.28.ids_i
  3.9 160.6 %siglip.1 = (bf16[2,192,1152]{2,1,0:T(8,128)(2,1)}, f32[1]{0:T(128)}) custom-call(bf16[144,192]{1,0:T(8,128)(2,1)} %fi.1, bf16[144,192]{1,0:T(8,128)(2,1)} %ft.1, bf16[192,1152]{1,0:T(8,128)(2,1)} %hi.1, bf16[192,1152]{1,0:T(8,128)(2,1)} %ht.1, s32[576,1]{1,0:T(8,128)} %reshape.28.ids_i, s32[1,768]{1,0:T(1,128)} %reshape.25.ids_t, f32[1]{0:T(128)S(6)} %copy.16.scale, ...), custom_call_target="tpu_custom_call" | custom-call | flops 4000000000 | bytes 10000000 | tf_op jit(solution)/shard_map/siglip/pallas_call | solution.py:615
  164.5 2.5 %bitcast_convert_fusion = (f32[192,1152]{1,0:T(8,128)}, f32[192,1152]{1,0:T(8,128)}) fusion(bf16[2,192,1152]{2,1,0:T(8,128)(2,1)} %get-tuple-element.6), kind=kLoop, calls=%fused_computation | loop fusion | flops 442368 | bytes 2654208 | tf_op jit(solution)/shard_map/convert_element_type | solution.py:638
  (2 shorter events, 0.0 us)
Async XLA Ops:
  0.6 1.4 copy-start
